TPU v7x, 32 devices: a whole 2x2x4 slice. The times are simulated.
32 devices in a mesh: clus: 4 (over y, x), wide: 8 (over z, core).
Axes of the slice: x: 2, y: 2, z: 4, core: 2. Of those that a mesh axis runs over, the one named last changes fastest.
Arguments:
- documents: bfloat16 [16384, 768], P(('clus', 'wide')), may hold values from -96 to 96
- source_device: int32 [4, 4096], P('clus', 'wide'), may hold values from 0 to 31, as said below
- source_row: int32 [4, 4096], P('clus', 'wide'), may hold values from 0 to 511
- centroids: float32 [4, 768], P('clus'), may hold values from -6 to 6
Outputs:
- nearest_earlier: float32 [4, 4096], P('clus', 'wide')
- centroid_distance: float32 [4, 4096], P('clus', 'wide')
Inputs may be any that keep to these rules, and one draw needn't show every extreme that they name: Together, (source_device, source_row) name every document row exactly once over all clusters. Among the 512 members of one device's block (members w * 512 to (w + 1) * 512 - 1 of a cluster) at most 32 come from one source device, and in every such block some source device supplies exactly 32.
All inputs are finite; a program needn't handle non-finite values.
Results may differ from a plain program's by a relative error of at most 0.0024.
Values may be sent and summed in bfloat16 or wider, within the bound.
A program may use at most 64 MiB of HBM per device.

v0:
```python
import jax
import jax.numpy as jnp
from jax import lax
from jax.sharding import PartitionSpec as P


def unit_rows(raw_rows):
    values = raw_rows.astype(jnp.float32)
    return values * lax.rsqrt(jnp.sum(values * values, axis=-1, keepdims=True) + 1e-06)


def inner_products(left_rows, right_rows):
    return lax.dot_general(
        left_rows, right_rows, (((1,), (1,)), ((), ())), preferred_element_type=jnp.float32
    )


def on_device(documents, source_device, source_row, centroids):
    devices = lax.axis_size(("clus", "wide"))
    members = source_device.shape[1]
    width = documents.shape[1]
    capacity = 2 * members // devices
    senders = source_device[0]
    picked_rows = source_row[0]
    counter = jnp.arange(members, dtype=jnp.int32)
    earlier_same = (senders[:, None] == senders[None, :]) & (counter[None, :] < counter[:, None])
    slots = jnp.sum(earlier_same.astype(jnp.int32), axis=1)
    places = senders * capacity + slots
    wanted = (
        jnp.zeros((devices * capacity,), jnp.int32)
        .at[places]
        .set(picked_rows)
        .reshape(devices, capacity)
    )
    asked = lax.all_to_all(wanted, ("clus", "wide"), split_axis=0, concat_axis=0, tiled=True)
    outgoing = jnp.take(documents, asked.reshape(-1), axis=0).reshape(devices, capacity, width)
    arrived = lax.all_to_all(outgoing, ("clus", "wide"), split_axis=0, concat_axis=0, tiled=True)
    gathered = jnp.take(arrived.reshape(devices * capacity, width), places, axis=0)
    normal_rows = unit_rows(gathered)
    direction = unit_rows(centroids)
    distance = 1.0 - jnp.sum(normal_rows * direction, axis=1)
    stored = normal_rows.astype(jnp.bfloat16)
    position = lax.axis_index("wide")
    first_row = position * members
    my_rows = first_row + counter
    initial = jnp.full((members,), -1.0, jnp.float32)
    piece = lax.all_gather(stored, "wide", axis=0, tiled=True)
    scores = inner_products(stored, piece)
    columns = jnp.arange(piece.shape[0], dtype=jnp.int32)
    scores = jnp.where(columns[None, :] < my_rows[:, None], scores, -1.0)
    nearest = jnp.maximum(initial, jnp.max(scores, axis=1))
    return (nearest[None, :], distance[None, :])


def solution(mesh):
    placed = (P(("clus", "wide"), None), P("clus", "wide"), P("clus", "wide"), P("clus", None))
    return jax.shard_map(
        on_device,
        mesh=mesh,
        in_specs=placed,
        out_specs=(P("clus", "wide"), P("clus", "wide")),
        check_vma=False,
    )
```

profile of v0, /device:TPU:0, one launch (start us, length us, event | category | flops | bytes accessed | tf_op | source)
XLA Modules:
  0.0 154.5 jit_solution(18010129880142255130)
XLA Ops:
  7.2 0.0 copy-start
  7.2 1.0 convert_reduce_fusion
  8.2 0.7 compare_select_fusion.2
  8.9 2.6 %scatter_custom_fusion = s32[1024]{0:T(1024)S(1)} fusion(s32[512]{0:T(512)S(1)} %bitcast.24, s32[512]{0:T(512)} %bitcast.28, s32[]{:T(128)} %constant.17.clone.1), kind=kCustom, calls=%fused_computation.27 | custom fusion | bytes 4608 | tf_op jit(solution)/shard_map/scatter | solution.py:32
  11.5 0.1 all_to_all.9
  11.6 14.2 %all_to_all.14 = s32[32,1,32]{2,1,0:T(1,128)S(1)} all-to-all(s32[32,1,32]{2,1,0:T(1,128)S(1)} %all_to_all.9), channel_id=1, replica_groups=mesh['clus'=4,'wide'=8] {'clus','wide'}, dimensions={0} | all-to-all | bytes 8192 | tf_op jit(solution)/shard_map/all_to_all | solution.py:35
  25.8 0.5 broadcast.107
  26.4 0.7 reduce.6
  27.1 0.1 reshape.132
  27.2 0.0 copy-done
  27.2 4.0 %gather_fusion = bf16[1024,768]{1,0:T(8,128)(2,1)S(1)} fusion(bf16[512,768]{1,0:T(8,128)(2,1)S(1)} %copy-done, s32[1024]{0:T(1024)S(1)} %broadcast_clamp_fusion), kind=kCustom, calls=%fused_computation | custom fusion | bytes 3149824 | tf_op jit(solution)/shard_map/jit(_take)/gather | solution.py:36
  31.2 1.4 broadcast_select_fusion
  32.6 0.0 copy-start.2
  32.6 0.0 copy-start.1
  32.6 2.8 %all-to-all-start.1 = ((bf16[32,32,768]{2,1,0:T(8,128)(2,1)}), bf16[32,32,768]{2,1,0:T(8,128)(2,1)S(1)}, u32[]{:S(2)}, u32[]{:S(2)}) async-start(bf16[32,32,768]{2,1,0:T(8,128)(2,1)} %broadcast_select_fusion), calls=%async_computation.1 | async-start | bytes 3145728 | tf_op jit(solution)/shard_map/all_to_all | solution.py:37
  35.4 0.0 all-gather.2.cloned.1.call-start
  35.4 0.0 copy-done.2
  35.4 0.6 multiply_reduce_fusion.1
  36.8 0.0 copy-done.1
  36.8 37.4 %all-to-all-done.1 = bf16[32,32,768]{2,1,0:T(8,128)(2,1)S(1)} async-done(((bf16[32,32,768]{2,1,0:T(8,128)(2,1)}), bf16[32,32,768]{2,1,0:T(8,128)(2,1)S(1)}, u32[]{:S(2)}, u32[]{:S(2)}) %all-to-all-start.1) | async-done | bytes 1572896 | tf_op jit(solution)/shard_map/all_to_all | solution.py:37
  74.3 2.0 %gather_fusion.1 = bf16[512,768]{1,0:T(8,128)(2,1)S(1)} fusion(bf16[1024,768]{1,0:T(8,128)(2,1)S(1)} %bitcast.17, s32[1024]{0:T(1024)S(1)} %pad_clamp_fusion), kind=kCustom, calls=%fused_computation.1 | custom fusion | bytes 1574912 | tf_op jit(solution)/shard_map/jit(_take)/gather | solution.py:38
  76.3 0.4 fusion.3
  76.7 1.3 fusion.2
  78.0 0.0 all-gather.2.cloned.1.call-update
  78.1 0.6 broadcast_subtract_fusion
  78.6 61.9 %all-gather.2.cloned.1.call-done = bf16[4096,768]{1,0:T(8,128)(2,1)} async-done(((bf16[512,768]{1,0:T(8,128)(2,1)}), bf16[4096,768]{1,0:T(8,128)(2,1)}) %all-gather.2.cloned.1.call-update) | async-done | bytes 6291472 | tf_op jit(solution)/shard_map/all_gather | solution.py:47
  140.5 6.6 %select_reduce_fusion = f32[512]{0:T(512)S(1)} fusion(bf16[512,768]{1,0:T(8,128)(2,1)} %get-tuple-element.3, bf16[4096,768]{1,0:T(8,128)(2,1)} %all-gather.2.cloned.1.call-done, s32[512]{0:T(512)S(1)} %iota_add_fusion), kind=kOutput, calls=%fused_computation.3 | convolution fusion | flops 3227516416 | bytes 7081984 | tf_op jit(solution)/shard_map/dot_general | solution.py:13
  147.1 0.6 broadcast_maximum_fusion
  (8 shorter events, 0.1 us)
Async XLA Ops:
  7.2 20.0 %copy-start = (bf16[512,768]{1,0:T(8,128)(2,1)S(1)}, bf16[512,768]{1,0:T(8,128)(2,1)}, u32[]{:S(2)}) copy-start(bf16[512,768]{1,0:T(8,128)(2,1)} %param.4) | copy-start | bytes 2359300
  32.6 2.9 %copy-start.2 = (f32[1,768]{1,0:T(1,128)S(1)}, f32[1,768]{1,0:T(1,128)}, u32[]{:S(2)}) copy-start(f32[1,768]{1,0:T(1,128)} %param.7) | copy-start | bytes 9220
  32.6 4.2 %copy-start.1 = (s32[1,512]{1,0:T(1,128)S(1)}, s32[1,512]{1,0:T(1,128)}, u32[]{:S(2)}) copy-start(s32[1,512]{1,0:T(1,128)} %param.5) | copy-start | bytes 6148
  32.6 41.7 %all-to-all-start.1 = ((bf16[32,32,768]{2,1,0:T(8,128)(2,1)}), bf16[32,32,768]{2,1,0:T(8,128)(2,1)S(1)}, u32[]{:S(2)}, u32[]{:S(2)}) async-start(bf16[32,32,768]{2,1,0:T(8,128)(2,1)} %broadcast_select_fusion), calls=%async_computation.1 | async-start | bytes 3145728 | tf_op jit(solution)/shard_map/all_to_all | solution.py:37
  35.4 105.1 %all-gather.2.cloned.1.call-start = ((), (), s32[]{:S(2)}) async-start(), calls=%async_computation.2 | async-start | bytes 7077888 | tf_op jit(solution)/shard_map/all_gather | solution.py:47
Sparse Core Ops, SparseCore 0:
  78.2 62.2 all-gather.1
where the time goes:
time: 155 us
  waiting for transfers between devices  99.3 us (64%)
  between operations  14.8 us (10%)
  blocking collectives  14.2 us (9%)
  local copies, waits for them, and re-layouts  9.32 us (6%)
  other arithmetic  7.34 us (5%)
  matrix products  6.6 us (4%)
  starting transfers between devices  2.86 us (2%)
    all_gather x1, waiting for transfers between devices, on_device(): piece = lax.all_gather(stored, 'wide', axis=0, tiled=True)  61.9 us
    all_to_all x1, waiting for transfers between devices, on_device(): lax.all_to_all(outgoing, ('clus', 'wide'), split_axis=0, concat_axis=0, t...  37.4 us
    all_to_all x1, blocking collectives, on_device(): lax.all_to_all(wanted, ('clus', 'wide'), split_axis=0, concat_axis=0, til...  14.2 us
    dot_general x1, matrix products, inner_products(): lax.dot_general(left_rows, right_rows, (((1,), (1,)), ((), ())), preferre...  6.6 us
    gather x1, local copies, waits for them, and re-layouts, on_device(): jnp.take(documents, asked.reshape(-1), axis=0)  4 us
  transfers between devices with their start and end apart: 2, of which 2 were waited for; matrix products, arithmetic and copies ran while one was open for 1% of the time, Pallas kernels for 0%

commit v1 on v0

v1 whole, which is shorter than its diff:
```python
import functools

import jax
import jax.numpy as jnp
from jax import lax
from jax.experimental import pallas as pl
from jax.experimental.pallas import tpu as pltpu
from jax.sharding import PartitionSpec as P

MESH = pl.DeviceIdType.MESH
LANES = 128


def iota(shape, dim):
    return lax.broadcasted_iota(jnp.int32, shape, dim)


def dot_nt(left, right):
    return lax.dot_general(
        left, right, (((1,), (1,)), ((), ())), preferred_element_type=jnp.float32
    )


def dot_nn(left, right):
    return jnp.dot(left, right, preferred_element_type=jnp.float32)


def as_column(row):
    return jnp.transpose(jnp.broadcast_to(row, (LANES, row.shape[1])))[:, :1]


def kernel(
    clusters, wide, cap, slots,
    docs_ref, sender_ref, row_ref, centroid_ref,
    near_ref, dist_ref,
    wanted, asked, place_out, place_in, cent_out, cent_in,
    outgoing, arrived, total, gathered, best, res_out, res_in,
    ask_send, ask_recv, info_send, info_recv, row_send, row_recv,
    block_send, block_recv, pass_send, res_send, res_recv,
):
    devices = clusters * wide
    members = sender_ref.shape[1]
    doc_rows, width = docs_ref.shape
    swapped = wide == 2 * clusters
    my_clus = lax.axis_index("clus")
    my_wide = lax.axis_index("wide")
    me = my_clus * wide + my_wide

    def role(device):
        if not swapped:
            return device
        first, rest = lax.div(device, wide), lax.rem(device, wide)
        return lax.div(rest, 2) * wide + 2 * first + lax.rem(rest, 2)

    def where_is(device):
        return (lax.div(device, wide), lax.rem(device, wide))

    def remote(src, dst, send, recv, device):
        return pltpu.make_async_remote_copy(
            src_ref=src, dst_ref=dst, send_sem=send, recv_sem=recv,
            device_id=where_is(device), device_id_type=MESH,
        )

    barrier = pltpu.get_barrier_semaphore()

    @pl.loop(1, devices)
    def _(t):
        other = lax.rem(me + t, devices)
        pl.semaphore_signal(barrier, inc=1, device_id=where_is(other), device_id_type=MESH)

    senders = sender_ref[...]
    same = iota((devices, members), 0) == senders
    one_hot = same.astype(jnp.float32)
    earlier = (iota((members, members), 0) < iota((members, members), 1)).astype(jnp.float32)
    rank = dot_nn(one_hot.astype(jnp.bfloat16), earlier.astype(jnp.bfloat16))
    slot = jnp.sum(jnp.where(same, rank, 0.0), axis=0, keepdims=True).astype(jnp.int32)
    place_out[...] = senders * slots + slot
    cent_out[...] = centroid_ref[...]
    at_slot = (iota((LANES, members), 0) == slot).astype(jnp.float32).astype(jnp.bfloat16)
    named = row_ref[...] + 1
    high = lax.shift_right_logical(named, 8)
    low = named - high * 256
    ask_low = dot_nt((one_hot * low.astype(jnp.float32)).astype(jnp.bfloat16), at_slot)
    ask_high = dot_nt((one_hot * high.astype(jnp.float32)).astype(jnp.bfloat16), at_slot)
    ask = (ask_low + 256.0 * ask_high).astype(jnp.int32)
    for s in range(devices):
        wanted[s] = ask[s:s + 1, :]

    pl.semaphore_wait(barrier, devices - 1)

    partner = role(me)
    asked[me] = wanted[me]

    @pl.loop(1, devices)
    def _(t):
        other = lax.rem(me + t, devices)
        remote(wanted.at[other], asked.at[me], ask_send.at[other], ask_recv.at[me], other).start()

    place_copy = remote(place_out, place_in, info_send.at[0], info_recv.at[0], partner)
    cent_copy = remote(cent_out, cent_in, info_send.at[1], info_recv.at[1], partner)

    @pl.when(partner != me)
    def _():
        place_copy.start()
        cent_copy.start()

    @pl.when(partner == me)
    def _():
        place_in[...] = place_out[...]
        cent_in[...] = cent_out[...]

    @pl.loop(1, devices)
    def _(t):
        other = lax.rem(me + devices - t, devices)
        remote(wanted.at[me], asked.at[other], ask_send.at[other], ask_recv.at[other], other).wait_recv()

    asked_t = jnp.transpose(asked[:, 0, :].astype(jnp.float32))
    doc_ids = (iota((slots, doc_rows), 1) + 1).astype(jnp.float32)
    docs = docs_ref[...]
    per_dot = max(1, LANES // slots)
    for first in range(0, devices, per_dot):
        chosen = jnp.concatenate(
            [
                (asked_t[:slots, o:o + 1] == doc_ids).astype(jnp.float32)
                for o in range(first, first + per_dot)
            ],
            axis=0,
        ).astype(jnp.bfloat16)
        rows = dot_nn(chosen, docs).astype(jnp.bfloat16)
        for i in range(per_dot):
            outgoing[first + i] = rows[i * slots:(i + 1) * slots]

    @pl.loop(1, devices)
    def _(t):
        holder = lax.rem(me + t, devices)
        remote(outgoing.at[role(holder)], arrived.at[me], row_send.at[holder], row_recv.at[me], holder).start()

    arrived[me] = outgoing[partner]

    @pl.when(partner != me)
    def _():
        place_copy.wait_recv()
        cent_copy.wait_recv()

    places = as_column(place_in[...].astype(jnp.float32))
    per_part = max(1, 256 // slots)
    for first in range(0, devices, per_part):
        for s in range(first, first + per_part):
            @pl.when(s != me)
            def _(s=s):
                remote(outgoing.at[s], arrived.at[s], row_send.at[s], row_recv.at[s], s).wait_recv()
        ids = (first * slots + iota((members, per_part * slots), 1)).astype(jnp.float32)
        pick = (places == ids).astype(jnp.float32).astype(jnp.bfloat16)
        part = dot_nn(pick, arrived[first:first + per_part].reshape(per_part * slots, width))
        if first == 0:
            total[...] = part
        else:
            total[...] += part

    block = lax.rem(partner, wide)
    cluster = lax.div(partner, wide)
    values = total[...]
    unit = values * lax.rsqrt(jnp.sum(values * values, axis=1, keepdims=True) + 1e-06)
    centroid = cent_in[...]
    direction = centroid * lax.rsqrt(jnp.sum(centroid * centroid, axis=1, keepdims=True) + 1e-06)
    distance = 1.0 - jnp.sum(unit * direction, axis=1, keepdims=True)
    gathered[block] = unit.astype(jnp.bfloat16)

    chips = wide // 2
    chip, core = lax.div(block, 2), lax.rem(block, 2)
    sibling = role(cluster * wide + 2 * chip + 1 - core)

    def holder_of(some_chip):
        return role(cluster * wide + 2 * some_chip + core)

    def block_copy(target_chip):
        return remote(gathered.at[block], gathered.at[block], block_send.at[target_chip],
                      block_recv.at[block], holder_of(target_chip))

    def sibling_copy(which):
        return remote(gathered.at[which], gathered.at[which], pass_send.at[which],
                      block_recv.at[which], sibling)

    @pl.loop(chip + 1, chips)
    def _(later):
        block_copy(later).start()

    @pl.when(core == 0)
    def _():
        sibling_copy(block).start()

    def fold(scores):
        out = scores[:, :LANES]
        for i in range(1, members // LANES):
            out = jnp.maximum(out, scores[:, i * LANES:(i + 1) * LANES])
        return out

    mine = gathered[block]
    scores = dot_nt(mine, mine)
    scores = jnp.where(iota((members, members), 1) < iota((members, members), 0), scores, -1.0)
    best[...] = jnp.maximum(fold(scores), -1.0)

    def meet(which):
        best[...] = jnp.maximum(best[...], fold(dot_nt(gathered[block], gathered[which])))

    @pl.when(core == 1)
    def _():
        sibling_copy(2 * chip).wait_recv()
        meet(2 * chip)

    @pl.loop(0, chip)
    def _(t):
        direct = 2 * (chip - 1 - t) + core
        sibling_copy(direct).wait_recv()
        sibling_copy(direct).start()
        meet(direct)
        passed = 2 * (chip - 1 - t) + 1 - core
        sibling_copy(passed).wait_recv()
        meet(passed)

    nearest = jnp.max(best[...], axis=1, keepdims=True)
    column = iota((members, LANES), 1)
    both = jnp.transpose(jnp.where(column == 0, nearest, distance))
    res_out[...] = both[:8]

    res_copy = remote(res_out, res_in, res_send, res_recv, partner)

    @pl.when(partner != me)
    def _():
        res_copy.start()
        res_copy.wait_recv()

    @pl.when(partner == me)
    def _():
        res_in[...] = res_out[...]

    near_ref[...] = res_in[0:1, :]
    dist_ref[...] = res_in[1:2, :]

    @pl.when(partner != me)
    def _():
        res_copy.wait_send()
        place_copy.wait_send()
        cent_copy.wait_send()

    @pl.loop(1, devices)
    def _(t):
        other = lax.rem(me + t, devices)
        remote(wanted.at[other], asked.at[me], ask_send.at[other], ask_recv.at[me], other).wait_send()
        remote(outgoing.at[other], arrived.at[me], row_send.at[other], row_recv.at[me], other).wait_send()

    @pl.loop(chip + 1, chips)
    def _(later):
        block_copy(later).wait_send()

    @pl.when(core == 0)
    def _():
        sibling_copy(block).wait_send()

    @pl.loop(0, chip)
    def _(t):
        sibling_copy(2 * (chip - 1 - t) + core).wait_send()


def solution(mesh):
    clusters, wide = mesh.shape["clus"], mesh.shape["wide"]
    devices = clusters * wide

    def on_device(documents, source_device, source_row, centroids):
        members = source_device.shape[1]
        width = documents.shape[1]
        cap = 2 * members // devices
        slots = max(16, cap)
        dma = pltpu.SemaphoreType.DMA
        f32, bf16, i32 = jnp.float32, jnp.bfloat16, jnp.int32
        vmem = pl.BlockSpec(memory_space=pltpu.VMEM)
        return pl.pallas_call(
            functools.partial(kernel, clusters, wide, cap, slots),
            out_shape=[jax.ShapeDtypeStruct((1, members), f32)] * 2,
            in_specs=[vmem] * 4,
            out_specs=[vmem] * 2,
            scratch_shapes=[
                pltpu.VMEM((devices, 1, LANES), i32),
                pltpu.VMEM((devices, 1, LANES), i32),
                pltpu.VMEM((1, members), i32),
                pltpu.VMEM((1, members), i32),
                pltpu.VMEM((1, width), f32),
                pltpu.VMEM((1, width), f32),
                pltpu.VMEM((devices, slots, width), bf16),
                pltpu.VMEM((devices, slots, width), bf16),
                pltpu.VMEM((members, width), f32),
                pltpu.VMEM((wide, members, width), bf16),
                pltpu.VMEM((members, LANES), f32),
                pltpu.VMEM((8, members), f32),
                pltpu.VMEM((8, members), f32),
                dma((devices,)), dma((devices,)), dma((2,)), dma((2,)),
                dma((devices,)), dma((devices,)),
                dma((wide // 2,)), dma((wide,)), dma((wide,)), dma, dma,
            ],
            compiler_params=pltpu.CompilerParams(
                collective_id=0, has_side_effects=True, vmem_limit_bytes=56 * 1024 * 1024
            ),
        )(documents, source_device, source_row, centroids)

    placed = (P(("clus", "wide"), None), P("clus", "wide"), P("clus", "wide"), P("clus", None))
    return jax.shard_map(
        on_device,
        mesh=mesh,
        in_specs=placed,
        out_specs=(P("clus", "wide"), P("clus", "wide")),
        check_vma=False,
    )
```

time: 155 us -> 94.3 us (0.61)
  the two profiles are of different devices: /device:TPU:0 before, /device:TPU:24 now
where the time goes in v1:
time: 94.3 us; the launch traced here: 94.1 us
  Pallas kernels  91.6 us (97%)
  local copies, waits for them, and re-layouts  1.89 us (2%)
    pallas_call x1, Pallas kernels, on_device(): pl.pallas_call(functools.partial(kernel, clusters, wide, cap, slots), out...  91.6 us
    unnamed x6, local copies, waits for them, and re-layouts  1.89 us

profile of v1, /device:TPU:24, one launch (start us, length us, event | category | flops | bytes accessed | tf_op | source)
XLA Modules:
  0.0 94.1 jit_solution(10734972545830949274)
XLA Ops:
  0.6 91.6 %shard_map.59 = (f32[1,512]{1,0:T(1,128)}, f32[1,512]{1,0:T(1,128)}) custom-call(bf16[512,768]{1,0:T(8,128)(2,1)} %docs_ref.1, s32[1,512]{1,0:T(1,128)} %sender_ref.1, s32[1,512]{1,0:T(1,128)} %row_ref.1, f32[1,768]{1,0:T(1,128)} %centroid_ref.1), custom_call_target="tpu_custom_call" | custom-call | tf_op jit(solution)/shard_map/pallas_call | solution.py:277
  92.2 0.0 copy-start.1
  92.2 0.7 copy-done.1
  92.9 0.0 copy-start
  92.9 0.6 copy.8
  93.4 0.1 copy-done
  93.5 0.6 copy.9
Async XLA Ops:
  92.2 0.7 copy-start.1
  92.9 0.7 copy-start

commit v2 on v1

--- a/solution.py
+++ b/solution.py
@@ -36,7 +36,7 @@
     wanted, asked, place_out, place_in, cent_out, cent_in,
     outgoing, arrived, total, gathered, best, res_out, res_in,
     ask_send, ask_recv, info_send, info_recv, row_send, row_recv,
-    block_send, block_recv, pass_send, res_send, res_recv,
+    block_send, block_recv, pass_send, relay_send, res_send, res_recv,
 ):
     devices = clusters * wide
     members = sender_ref.shape[1]
@@ -181,9 +181,29 @@
         return remote(gathered.at[which], gathered.at[which], pass_send.at[which],
                       block_recv.at[which], sibling)
 
+    relayed = swapped and chips == 4
+
+    def goes_direct(later):
+        if not relayed:
+            return later >= 0
+        by_third = ((chip == 0) & (later == 3)) | ((chip == 1) & (later == 2) & (core == 1))
+        return jnp.logical_not(by_third)
+
+    relay_block = jnp.where(chip == 1, 0, jnp.where(chip == 2, 1, 3))
+    relays = ((chip == 1) & (core == 0)) | ((chip >= 2) & (core == 1))
+    relay_copy = remote(gathered.at[relay_block], gathered.at[relay_block], relay_send,
+                        block_recv.at[relay_block], holder_of(jnp.where(chip == 3, 2, 3)))
+
+    def source_chip(t):
+        if not relayed:
+            return chip - 1 - t
+        return jnp.where(chip == 2, t, chip - 1 - t)
+
     @pl.loop(chip + 1, chips)
     def _(later):
-        block_copy(later).start()
+        @pl.when(goes_direct(later))
+        def _():
+            block_copy(later).start()
 
     @pl.when(core == 0)
     def _():
@@ -210,11 +230,15 @@
 
     @pl.loop(0, chip)
     def _(t):
-        direct = 2 * (chip - 1 - t) + core
+        direct = 2 * source_chip(t) + core
         sibling_copy(direct).wait_recv()
+        if relayed:
+            @pl.when(relays & (direct == relay_block))
+            def _():
+                relay_copy.start()
         sibling_copy(direct).start()
         meet(direct)
-        passed = 2 * (chip - 1 - t) + 1 - core
+        passed = 2 * source_chip(t) + 1 - core
         sibling_copy(passed).wait_recv()
         meet(passed)
 
@@ -251,7 +275,14 @@
 
     @pl.loop(chip + 1, chips)
     def _(later):
-        block_copy(later).wait_send()
+        @pl.when(goes_direct(later))
+        def _():
+            block_copy(later).wait_send()
+
+    if relayed:
+        @pl.when(relays)
+        def _():
+            relay_copy.wait_send()
 
     @pl.when(core == 0)
     def _():
@@ -295,7 +326,7 @@
                 pltpu.VMEM((8, members), f32),
                 dma((devices,)), dma((devices,)), dma((2,)), dma((2,)),
                 dma((devices,)), dma((devices,)),
-                dma((wide // 2,)), dma((wide,)), dma((wide,)), dma, dma,
+                dma((wide // 2,)), dma((wide,)), dma((wide,)), dma, dma, dma,
             ],
             compiler_params=pltpu.CompilerParams(
                 collective_id=0, has_side_effects=True, vmem_limit_bytes=56 * 1024 * 1024

time: 94.3 us -> 95.3 us (1.011)
  Pallas kernels: 91.6 us -> 92.6 us
    pallas_call x1, Pallas kernels: 91.6 us -> 92.6 us  [on_device(): pl.pallas_call(functools.partial(kernel, clusters, wide, cap, slots), out...]
where the time goes in v2:
time: 95.3 us; the launch traced here: 95.1 us
  Pallas kernels  92.6 us (97%)
  local copies, waits for them, and re-layouts  1.89 us (2%)
    pallas_call x1, Pallas kernels, on_device(): pl.pallas_call(functools.partial(kernel, clusters, wide, cap, slots), out...  92.6 us

profile of v2, /device:TPU:24, one launch (start us, length us, event | category | flops | bytes accessed | tf_op | source)
XLA Modules:
  0.0 95.1 jit_solution(16118346988647086235)
XLA Ops:
  0.6 92.6 %shard_map.59 = (f32[1,512]{1,0:T(1,128)}, f32[1,512]{1,0:T(1,128)}) custom-call(bf16[512,768]{1,0:T(8,128)(2,1)} %docs_ref.1, s32[1,512]{1,0:T(1,128)} %sender_ref.1, s32[1,512]{1,0:T(1,128)} %row_ref.1, f32[1,768]{1,0:T(1,128)} %centroid_ref.1), custom_call_target="tpu_custom_call" | custom-call | tf_op jit(solution)/shard_map/pallas_call | solution.py:308
  93.2 0.0 copy-start.1
  93.2 0.7 copy-done.1
  93.9 0.0 copy-start
  93.9 0.6 copy.8
  94.5 0.1 copy-done
  94.5 0.6 copy.9
Async XLA Ops:
  93.2 0.7 copy-start.1
  93.9 0.7 copy-start

commit v3 on v1

--- a/solution.py
+++ b/solution.py
@@ -164,7 +164,10 @@
     centroid = cent_in[...]
     direction = centroid * lax.rsqrt(jnp.sum(centroid * centroid, axis=1, keepdims=True) + 1e-06)
     distance = 1.0 - jnp.sum(unit * direction, axis=1, keepdims=True)
-    gathered[block] = unit.astype(jnp.bfloat16)
+    mine = unit.astype(jnp.bfloat16)
+    half = members // 2
+    gathered[2 * block] = mine[:half]
+    gathered[2 * block + 1] = mine[half:]
 
     chips = wide // 2
     chip, core = lax.div(block, 2), lax.rem(block, 2)
@@ -173,9 +176,10 @@
     def holder_of(some_chip):
         return role(cluster * wide + 2 * some_chip + core)
 
-    def block_copy(target_chip):
-        return remote(gathered.at[block], gathered.at[block], block_send.at[target_chip],
-                      block_recv.at[block], holder_of(target_chip))
+    def block_copy(target_chip, h):
+        part = 2 * block + h
+        return remote(gathered.at[part], gathered.at[part], block_send.at[2 * target_chip + h],
+                      block_recv.at[part], holder_of(target_chip))
 
     def sibling_copy(which):
         return remote(gathered.at[which], gathered.at[which], pass_send.at[which],
@@ -183,40 +187,46 @@
 
     @pl.loop(chip + 1, chips)
     def _(later):
-        block_copy(later).start()
+        block_copy(later, 0).start()
+
+    @pl.loop(chip + 1, chips)
+    def _(later):
+        block_copy(later, 1).start()
 
     @pl.when(core == 0)
     def _():
-        sibling_copy(block).start()
+        sibling_copy(2 * block).start()
+        sibling_copy(2 * block + 1).start()
 
     def fold(scores):
         out = scores[:, :LANES]
-        for i in range(1, members // LANES):
+        for i in range(1, scores.shape[1] // LANES):
             out = jnp.maximum(out, scores[:, i * LANES:(i + 1) * LANES])
         return out
 
-    mine = gathered[block]
     scores = dot_nt(mine, mine)
     scores = jnp.where(iota((members, members), 1) < iota((members, members), 0), scores, -1.0)
     best[...] = jnp.maximum(fold(scores), -1.0)
 
     def meet(which):
-        best[...] = jnp.maximum(best[...], fold(dot_nt(gathered[block], gathered[which])))
+        best[...] = jnp.maximum(best[...], fold(dot_nt(gathered[pl.ds(2 * block, 2)].reshape(members, width), gathered[which])))
 
     @pl.when(core == 1)
     def _():
-        sibling_copy(2 * chip).wait_recv()
-        meet(2 * chip)
-
-    @pl.loop(0, chip)
-    def _(t):
-        direct = 2 * (chip - 1 - t) + core
-        sibling_copy(direct).wait_recv()
-        sibling_copy(direct).start()
-        meet(direct)
-        passed = 2 * (chip - 1 - t) + 1 - core
-        sibling_copy(passed).wait_recv()
-        meet(passed)
+        for h in range(2):
+            sibling_copy(4 * chip + h).wait_recv()
+            meet(4 * chip + h)
+
+    for h in range(2):
+        @pl.loop(0, chip)
+        def _(t, h=h):
+            direct = 2 * (2 * (chip - 1 - t) + core) + h
+            sibling_copy(direct).wait_recv()
+            sibling_copy(direct).start()
+            meet(direct)
+            passed = 2 * (2 * (chip - 1 - t) + 1 - core) + h
+            sibling_copy(passed).wait_recv()
+            meet(passed)
 
     nearest = jnp.max(best[...], axis=1, keepdims=True)
     column = iota((members, LANES), 1)
@@ -251,15 +261,18 @@
 
     @pl.loop(chip + 1, chips)
     def _(later):
-        block_copy(later).wait_send()
+        block_copy(later, 0).wait_send()
+        block_copy(later, 1).wait_send()
 
     @pl.when(core == 0)
     def _():
-        sibling_copy(block).wait_send()
+        sibling_copy(2 * block).wait_send()
+        sibling_copy(2 * block + 1).wait_send()
 
     @pl.loop(0, chip)
     def _(t):
-        sibling_copy(2 * (chip - 1 - t) + core).wait_send()
+        for h in range(2):
+            sibling_copy(2 * (2 * (chip - 1 - t) + core) + h).wait_send()
 
 
 def solution(mesh):
@@ -289,13 +302,13 @@
                 pltpu.VMEM((devices, slots, width), bf16),
                 pltpu.VMEM((devices, slots, width), bf16),
                 pltpu.VMEM((members, width), f32),
-                pltpu.VMEM((wide, members, width), bf16),
+                pltpu.VMEM((2 * wide, members // 2, width), bf16),
                 pltpu.VMEM((members, LANES), f32),
                 pltpu.VMEM((8, members), f32),
                 pltpu.VMEM((8, members), f32),
                 dma((devices,)), dma((devices,)), dma((2,)), dma((2,)),
                 dma((devices,)), dma((devices,)),
-                dma((wide // 2,)), dma((wide,)), dma((wide,)), dma, dma,
+                dma((wide,)), dma((2 * wide,)), dma((2 * wide,)), dma, dma,
             ],
             compiler_params=pltpu.CompilerParams(
                 collective_id=0, has_side_effects=True, vmem_limit_bytes=56 * 1024 * 1024

time: 94.3 us -> 94.1 us (level)
  no operation moved by 1% of the time
where the time goes in v3:
time: 94.1 us; the launch traced here: 93.9 us
  Pallas kernels  91.3 us (97%)
  local copies, waits for them, and re-layouts  1.89 us (2%)
    pallas_call x1, Pallas kernels, on_device(): pl.pallas_call(functools.partial(kernel, clusters, wide, cap, slots), out...  91.3 us
    unnamed x6, local copies, waits for them, and re-layouts  1.89 us

profile of v3, /device:TPU:24, one launch (start us, length us, event | category | flops | bytes accessed | tf_op | source)
XLA Modules:
  0.0 93.9 jit_solution(16647558538449902416)
XLA Ops:
  0.6 91.3 %shard_map.59 = (f32[1,512]{1,0:T(1,128)}, f32[1,512]{1,0:T(1,128)}) custom-call(bf16[512,768]{1,0:T(8,128)(2,1)} %docs_ref.1, s32[1,512]{1,0:T(1,128)} %sender_ref.1, s32[1,512]{1,0:T(1,128)} %row_ref.1, f32[1,768]{1,0:T(1,128)} %centroid_ref.1), custom_call_target="tpu_custom_call" | custom-call | tf_op jit(solution)/shard_map/pallas_call | solution.py:290
  92.0 0.0 copy-start.1
  92.0 0.7 copy-done.1
  92.6 0.0 copy-start
  92.6 0.6 copy.8
  93.2 0.1 copy-done
  93.3 0.6 copy.9
Async XLA Ops:
  92.0 0.7 copy-start.1
  92.6 0.7 copy-start

commit v4 on v1

--- a/solution.py
+++ b/solution.py
@@ -34,13 +34,14 @@
     docs_ref, sender_ref, row_ref, centroid_ref,
     near_ref, dist_ref,
     wanted, asked, place_out, place_in, cent_out, cent_in,
-    outgoing, arrived, total, gathered, best, res_out, res_in,
+    outgoing, arrived, total, gathered, own, scales, best, res_out, res_in,
     ask_send, ask_recv, info_send, info_recv, row_send, row_recv,
-    block_send, block_recv, pass_send, res_send, res_recv,
+    block_send, block_recv, pass_send, scale_send, scale_recv, res_send, res_recv,
 ):
     devices = clusters * wide
     members = sender_ref.shape[1]
     doc_rows, width = docs_ref.shape
+    part = width // 2
     swapped = wide == 2 * clusters
     my_clus = lax.axis_index("clus")
     my_wide = lax.axis_index("wide")
@@ -128,14 +129,28 @@
         ).astype(jnp.bfloat16)
         rows = dot_nn(chosen, docs).astype(jnp.bfloat16)
         for i in range(per_dot):
-            outgoing[first + i] = rows[i * slots:(i + 1) * slots]
-
-    @pl.loop(1, devices)
-    def _(t):
-        holder = lax.rem(me + t, devices)
-        remote(outgoing.at[role(holder)], arrived.at[me], row_send.at[holder], row_recv.at[me], holder).start()
+            outgoing[first + i] = rows[i * slots:(i + 1) * slots, :part]
+            outgoing[devices + first + i] = rows[i * slots:(i + 1) * slots, part:]
+
+    def row_copy(holder, h):
+        return remote(outgoing.at[h * devices + role(holder)], arrived.at[h * devices + me],
+                      row_send.at[h * devices + holder], row_recv.at[h * devices + me], holder)
+
+    def row_arrival(source, h):
+        at = h * devices + source
+        return remote(outgoing.at[at], arrived.at[at], row_send.at[at], row_recv.at[at], source)
+
+    @pl.loop(1, devices)
+    def _(t):
+        row_copy(lax.rem(me + t, devices), 0).start()
 
     arrived[me] = outgoing[partner]
+    arrived[devices + me] = outgoing[devices + partner]
+
+    @pl.loop(1, devices)
+    def _(t):
+        row_copy(lax.rem(me + t, devices), 0).wait_send()
+        row_copy(lax.rem(me + t, devices), 1).start()
 
     @pl.when(partner != me)
     def _():
@@ -144,50 +159,75 @@
 
     places = as_column(place_in[...].astype(jnp.float32))
     per_part = max(1, 256 // slots)
-    for first in range(0, devices, per_part):
-        for s in range(first, first + per_part):
-            @pl.when(s != me)
-            def _(s=s):
-                remote(outgoing.at[s], arrived.at[s], row_send.at[s], row_recv.at[s], s).wait_recv()
-        ids = (first * slots + iota((members, per_part * slots), 1)).astype(jnp.float32)
-        pick = (places == ids).astype(jnp.float32).astype(jnp.bfloat16)
-        part = dot_nn(pick, arrived[first:first + per_part].reshape(per_part * slots, width))
-        if first == 0:
-            total[...] = part
-        else:
-            total[...] += part
+
+    def collect(h):
+        for first in range(0, devices, per_part):
+            for s in range(first, first + per_part):
+                @pl.when(s != me)
+                def _(s=s):
+                    row_arrival(s, h).wait_recv()
+            ids = (first * slots + iota((members, per_part * slots), 1)).astype(jnp.float32)
+            pick = (places == ids).astype(jnp.float32).astype(jnp.bfloat16)
+            base = h * devices + first
+            found = dot_nn(pick, arrived[base:base + per_part].reshape(per_part * slots, part))
+            if first == 0:
+                total[h] = found
+            else:
+                total[h] += found
 
     block = lax.rem(partner, wide)
     cluster = lax.div(partner, wide)
-    values = total[...]
-    unit = values * lax.rsqrt(jnp.sum(values * values, axis=1, keepdims=True) + 1e-06)
-    centroid = cent_in[...]
-    direction = centroid * lax.rsqrt(jnp.sum(centroid * centroid, axis=1, keepdims=True) + 1e-06)
-    distance = 1.0 - jnp.sum(unit * direction, axis=1, keepdims=True)
-    gathered[block] = unit.astype(jnp.bfloat16)
-
     chips = wide // 2
     chip, core = lax.div(block, 2), lax.rem(block, 2)
     sibling = role(cluster * wide + 2 * chip + 1 - core)
 
-    def holder_of(some_chip):
-        return role(cluster * wide + 2 * some_chip + core)
-
-    def block_copy(target_chip):
-        return remote(gathered.at[block], gathered.at[block], block_send.at[target_chip],
-                      block_recv.at[block], holder_of(target_chip))
-
-    def sibling_copy(which):
-        return remote(gathered.at[which], gathered.at[which], pass_send.at[which],
-                      block_recv.at[which], sibling)
-
-    @pl.loop(chip + 1, chips)
-    def _(later):
-        block_copy(later).start()
-
-    @pl.when(core == 0)
-    def _():
-        sibling_copy(block).start()
+    def block_copy(target_chip, h):
+        at = h * wide + block
+        return remote(gathered.at[at], gathered.at[at], block_send.at[h * chips + target_chip],
+                      block_recv.at[at], role(cluster * wide + 2 * target_chip + core))
+
+    def sibling_copy(which, h):
+        at = h * wide + which
+        return remote(gathered.at[at], gathered.at[at], pass_send.at[at], block_recv.at[at], sibling)
+
+    def scale_copy(which, target):
+        return remote(scales.at[which], scales.at[which], scale_send.at[target],
+                      scale_recv.at[which], role(cluster * wide + target))
+
+    def send_block(h):
+        @pl.loop(chip + 1, chips)
+        def _(later):
+            block_copy(later, h).start()
+
+        @pl.when(core == 0)
+        def _():
+            sibling_copy(block, h).start()
+
+    collect(0)
+    gathered[block] = total[0].astype(jnp.bfloat16)
+    send_block(0)
+
+    collect(1)
+    left, right = total[0], total[1]
+    squares = jnp.sum(left * left, axis=1, keepdims=True) + jnp.sum(right * right, axis=1, keepdims=True)
+    scale = lax.rsqrt(squares + 1e-06)
+    scales[block] = jnp.transpose(jnp.broadcast_to(scale, (members, LANES)))[:1]
+
+    @pl.loop(block + 1, wide)
+    def _(target):
+        scale_copy(block, target).start()
+
+    left, right = left * scale, right * scale
+    gathered[wide + block] = right.astype(jnp.bfloat16)
+    send_block(1)
+    own[...] = left.astype(jnp.bfloat16)
+
+    centroid = cent_in[...]
+    direction = centroid * lax.rsqrt(jnp.sum(centroid * centroid, axis=1, keepdims=True) + 1e-06)
+    distance = 1.0 - (
+        jnp.sum(left * direction[:, :part], axis=1, keepdims=True)
+        + jnp.sum(right * direction[:, part:], axis=1, keepdims=True)
+    )
 
     def fold(scores):
         out = scores[:, :LANES]
@@ -195,27 +235,39 @@
             out = jnp.maximum(out, scores[:, i * LANES:(i + 1) * LANES])
         return out
 
-    mine = gathered[block]
-    scores = dot_nt(mine, mine)
+    mine = gathered[wide + block]
+    scores = dot_nt(own[...], own[...]) + dot_nt(mine, mine)
     scores = jnp.where(iota((members, members), 1) < iota((members, members), 0), scores, -1.0)
     best[...] = jnp.maximum(fold(scores), -1.0)
 
     def meet(which):
-        best[...] = jnp.maximum(best[...], fold(dot_nt(gathered[block], gathered[which])))
+        scale_copy(which, block).wait_recv()
+        first_half = gathered[which].astype(jnp.float32) * as_column(scales[which])
+        scores = dot_nt(own[...], first_half.astype(jnp.bfloat16))
+        scores += dot_nt(gathered[wide + block], gathered[wide + which])
+        best[...] = jnp.maximum(best[...], fold(scores))
+
+    @pl.loop(0, chip)
+    def _(t):
+        direct = 2 * (chip - 1 - t) + core
+        sibling_copy(direct, 0).wait_recv()
+        sibling_copy(direct, 0).start()
 
     @pl.when(core == 1)
     def _():
-        sibling_copy(2 * chip).wait_recv()
+        sibling_copy(2 * chip, 0).wait_recv()
+        sibling_copy(2 * chip, 1).wait_recv()
         meet(2 * chip)
 
     @pl.loop(0, chip)
     def _(t):
         direct = 2 * (chip - 1 - t) + core
-        sibling_copy(direct).wait_recv()
-        sibling_copy(direct).start()
+        sibling_copy(direct, 1).wait_recv()
+        sibling_copy(direct, 1).start()
         meet(direct)
         passed = 2 * (chip - 1 - t) + 1 - core
-        sibling_copy(passed).wait_recv()
+        sibling_copy(passed, 0).wait_recv()
+        sibling_copy(passed, 1).wait_recv()
         meet(passed)
 
     nearest = jnp.max(best[...], axis=1, keepdims=True)
@@ -247,19 +299,27 @@
     def _(t):
         other = lax.rem(me + t, devices)
         remote(wanted.at[other], asked.at[me], ask_send.at[other], ask_recv.at[me], other).wait_send()
-        remote(outgoing.at[other], arrived.at[me], row_send.at[other], row_recv.at[me], other).wait_send()
+        row_copy(other, 1).wait_send()
 
     @pl.loop(chip + 1, chips)
     def _(later):
-        block_copy(later).wait_send()
+        block_copy(later, 0).wait_send()
+        block_copy(later, 1).wait_send()
 
     @pl.when(core == 0)
     def _():
-        sibling_copy(block).wait_send()
+        sibling_copy(block, 0).wait_send()
+        sibling_copy(block, 1).wait_send()
 
     @pl.loop(0, chip)
     def _(t):
-        sibling_copy(2 * (chip - 1 - t) + core).wait_send()
+        direct = 2 * (chip - 1 - t) + core
+        sibling_copy(direct, 0).wait_send()
+        sibling_copy(direct, 1).wait_send()
+
+    @pl.loop(block + 1, wide)
+    def _(target):
+        scale_copy(block, target).wait_send()
 
 
 def solution(mesh):
@@ -286,16 +346,19 @@
                 pltpu.VMEM((1, members), i32),
                 pltpu.VMEM((1, width), f32),
                 pltpu.VMEM((1, width), f32),
-                pltpu.VMEM((devices, slots, width), bf16),
-                pltpu.VMEM((devices, slots, width), bf16),
-                pltpu.VMEM((members, width), f32),
-                pltpu.VMEM((wide, members, width), bf16),
+                pltpu.VMEM((2 * devices, slots, width // 2), bf16),
+                pltpu.VMEM((2 * devices, slots, width // 2), bf16),
+                pltpu.VMEM((2, members, width // 2), f32),
+                pltpu.VMEM((2 * wide, members, width // 2), bf16),
+                pltpu.VMEM((members, width // 2), bf16),
+                pltpu.VMEM((wide, 1, members), f32),
                 pltpu.VMEM((members, LANES), f32),
                 pltpu.VMEM((8, members), f32),
                 pltpu.VMEM((8, members), f32),
                 dma((devices,)), dma((devices,)), dma((2,)), dma((2,)),
-                dma((devices,)), dma((devices,)),
-                dma((wide // 2,)), dma((wide,)), dma((wide,)), dma, dma,
+                dma((2 * devices,)), dma((2 * devices,)),
+                dma((wide,)), dma((2 * wide,)), dma((2 * wide,)),
+                dma((wide,)), dma((wide,)), dma, dma,
             ],
             compiler_params=pltpu.CompilerParams(
                 collective_id=0, has_side_effects=True, vmem_limit_bytes=56 * 1024 * 1024

time: 94.3 us -> 89.7 us (0.951)
  the two profiles are of different devices: /device:TPU:24 before, /device:TPU:26 now
where the time goes in v4:
time: 89.7 us; the launch traced here: 89.5 us
  Pallas kernels  87 us (97%)
  local copies, waits for them, and re-layouts  1.89 us (2%)
    pallas_call x1, Pallas kernels, on_device(): pl.pallas_call(functools.partial(kernel, clusters, wide, cap, slots), out...  87 us
    unnamed x6, local copies, waits for them, and re-layouts  1.89 us

profile of v4, /device:TPU:26, one launch (start us, length us, event | category | flops | bytes accessed | tf_op | source)
XLA Modules:
  0.0 89.5 jit_solution(10628715027961879114)
XLA Ops:
  0.6 87.0 %shard_map.59 = (f32[1,512]{1,0:T(1,128)}, f32[1,512]{1,0:T(1,128)}) custom-call(bf16[512,768]{1,0:T(8,128)(2,1)} %docs_ref.1, s32[1,512]{1,0:T(1,128)} %sender_ref.1, s32[1,512]{1,0:T(1,128)} %row_ref.1, f32[1,768]{1,0:T(1,128)} %centroid_ref.1), custom_call_target="tpu_custom_call" | custom-call | tf_op jit(solution)/shard_map/pallas_call | solution.py:337
  87.6 0.0 copy-start.1
  87.6 0.7 copy-done.1
  88.3 0.0 copy-start
  88.3 0.6 copy.8
  88.9 0.1 copy-done
  88.9 0.6 copy.9
Async XLA Ops:
  87.6 0.7 copy-start.1
  88.3 0.7 copy-start

commit v5 on v4

--- a/solution.py
+++ b/solution.py
@@ -140,17 +140,19 @@
         at = h * devices + source
         return remote(outgoing.at[at], arrived.at[at], row_send.at[at], row_recv.at[at], source)
 
-    @pl.loop(1, devices)
-    def _(t):
-        row_copy(lax.rem(me + t, devices), 0).start()
+    stride = 5 if devices % 5 else 1
+
+    @pl.loop(1, devices)
+    def _(t):
+        row_copy(lax.rem(me + stride * t, devices), 0).start()
 
     arrived[me] = outgoing[partner]
     arrived[devices + me] = outgoing[devices + partner]
 
     @pl.loop(1, devices)
     def _(t):
-        row_copy(lax.rem(me + t, devices), 0).wait_send()
-        row_copy(lax.rem(me + t, devices), 1).start()
+        row_copy(lax.rem(me + stride * t, devices), 0).wait_send()
+        row_copy(lax.rem(me + stride * t, devices), 1).start()
 
     @pl.when(partner != me)
     def _():

time: 89.7 us -> 87.1 us (0.971)
  the two profiles are of different devices: /device:TPU:26 before, /device:TPU:24 now
where the time goes in v5:
time: 87.1 us; the launch traced here: 85.3 us
  Pallas kernels  82.8 us (95%)
  local copies, waits for them, and re-layouts  1.89 us (2%)
    pallas_call x1, Pallas kernels, on_device(): pl.pallas_call(functools.partial(kernel, clusters, wide, cap, slots), out...  82.8 us
    unnamed x6, local copies, waits for them, and re-layouts  1.89 us

profile of v5, /device:TPU:24, one launch (start us, length us, event | category | flops | bytes accessed | tf_op | source)
XLA Modules:
  0.0 85.3 jit_solution(12483374902248786553)
XLA Ops:
  0.6 82.8 %shard_map.59 = (f32[1,512]{1,0:T(1,128)}, f32[1,512]{1,0:T(1,128)}) custom-call(bf16[512,768]{1,0:T(8,128)(2,1)} %docs_ref.1, s32[1,512]{1,0:T(1,128)} %sender_ref.1, s32[1,512]{1,0:T(1,128)} %row_ref.1, f32[1,768]{1,0:T(1,128)} %centroid_ref.1), custom_call_target="tpu_custom_call" | custom-call | tf_op jit(solution)/shard_map/pallas_call | solution.py:339
  83.4 0.0 copy-start.1
  83.5 0.7 copy-done.1
  84.1 0.0 copy-start
  84.1 0.6 copy.8
  84.7 0.1 copy-done
  84.8 0.6 copy.9
Async XLA Ops:
  83.4 0.7 copy-start.1
  84.1 0.7 copy-start

commit v6 on v5

--- a/solution.py
+++ b/solution.py
@@ -151,7 +151,6 @@
 
     @pl.loop(1, devices)
     def _(t):
-        row_copy(lax.rem(me + stride * t, devices), 0).wait_send()
         row_copy(lax.rem(me + stride * t, devices), 1).start()
 
     @pl.when(partner != me)
@@ -199,7 +198,7 @@
     def send_block(h):
         @pl.loop(chip + 1, chips)
         def _(later):
-            block_copy(later, h).start()
+            block_copy(chips + chip - later, h).start()
 
         @pl.when(core == 0)
         def _():
@@ -301,6 +300,7 @@
     def _(t):
         other = lax.rem(me + t, devices)
         remote(wanted.at[other], asked.at[me], ask_send.at[other], ask_recv.at[me], other).wait_send()
+        row_copy(other, 0).wait_send()
         row_copy(other, 1).wait_send()
 
     @pl.loop(chip + 1, chips)

time: 87.1 us -> 87.4 us (level); the launches traced: 85.3 us -> 87.2 us
  Pallas kernels: 82.8 us -> 84.6 us
    pallas_call x1, Pallas kernels: 82.8 us -> 84.6 us  [on_device(): pl.pallas_call(functools.partial(kernel, clusters, wide, cap, slots), out...]
where the time goes in v6:
time: 87.4 us; the launch traced here: 87.2 us
  Pallas kernels  84.6 us (97%)
  local copies, waits for them, and re-layouts  1.89 us (2%)
    pallas_call x1, Pallas kernels, on_device(): pl.pallas_call(functools.partial(kernel, clusters, wide, cap, slots), out...  84.6 us
    unnamed x6, local copies, waits for them, and re-layouts  1.89 us

profile of v6, /device:TPU:24, one launch (start us, length us, event | category | flops | bytes accessed | tf_op | source)
XLA Modules:
  0.0 87.2 jit_solution(13371197295458822238)
XLA Ops:
  0.6 84.6 %shard_map.59 = (f32[1,512]{1,0:T(1,128)}, f32[1,512]{1,0:T(1,128)}) custom-call(bf16[512,768]{1,0:T(8,128)(2,1)} %docs_ref.1, s32[1,512]{1,0:T(1,128)} %sender_ref.1, s32[1,512]{1,0:T(1,128)} %row_ref.1, f32[1,768]{1,0:T(1,128)} %centroid_ref.1), custom_call_target="tpu_custom_call" | custom-call | tf_op jit(solution)/shard_map/pallas_call | solution.py:339
  85.3 0.0 copy-start.1
  85.3 0.7 copy-done.1
  85.9 0.0 copy-start
  85.9 0.6 copy.8
  86.5 0.1 copy-done
  86.6 0.6 copy.9
Async XLA Ops:
  85.3 0.7 copy-start.1
  85.9 0.7 copy-start
